TPU v7x, 32 devices: a whole 2x2x4 slice. The times are simulated.
32 devices in a mesh: src: 16 (over z, y, x), fac: 2 (over core).
Axes of the slice: x: 2, y: 2, z: 4, core: 2. Of those that a mesh axis runs over, the one named last changes fastest.
Arguments:
- lower_inverse: bfloat16 [2, 1024, 2, 1024], P('fac', 'src'), as said below
- coupling: bfloat16 [2, 1024, 2, 1024], P('fac', 'src'), as said below
- source_cell: int32 [2048], P('src'), may hold values from 0 to 2047
- source_wave: float32 [2048, 2], P('src'), may hold values from -6 to 6
- inflow_field: bfloat16 [2048, 2, 1024], P('src'), may hold values from -6 to 6
- receiver_cell: int32 [2048, 128], P('src'), may hold values from 0 to 2047
- observed: float32 [2048, 2, 128], P('src'), may hold values from -6 to 6
- adjoint: bfloat16 [2048, 2, 2, 1024], P('src', 'fac'), may hold values from -6 to 6
Outputs:
- wavefield: float32 [2048, 2, 2, 1024], P('src', 'fac')
- data_residual: float32 [2048, 2, 128], P('src')
- gradient: float32 [2, 1024], P('fac', 'src')
Inputs may be any that keep to these rules, and one draw needn't show every extreme that they name: lower_inverse[i, j, p, k] is zero where k > j. coupling[i, j, p, k] is zero where k < j.
All inputs are finite; a program needn't handle non-finite values.
Results may differ from a plain program's by a relative error of at most 0.025.
Values may be sent and summed in bfloat16 or wider, within the bound.
A program may use at most 64 MiB of HBM per device.

v0:
```python
import math

import jax
import jax.numpy as jnp
from jax import lax
from jax.sharding import PartitionSpec as P


def from_behind(shard, axis, by):
    size = lax.axis_size(axis)
    pairs = [(i, i + by) for i in range(size) if 0 <= i + by < size]
    return lax.ppermute(shard, axis, pairs)


def complex_apply(vector, matrix):
    width = matrix.shape[0]
    joined = matrix.reshape(width, 2 * width)
    real_row = jnp.concatenate([vector[:, 0], -vector[:, 1]], axis=1)
    imag_row = jnp.concatenate([vector[:, 1], vector[:, 0]], axis=1)
    stacked = jnp.stack([real_row, imag_row], axis=1).reshape(-1, 2 * width)
    contract_dims = (((1,), (1,)), ((), ()))
    result = lax.dot_general(stacked, joined, contract_dims, preferred_element_type=jnp.float32)
    return result.reshape(vector.shape[0], 2, width)


def source_block(cells, wave, owner, width):
    cell_ids = owner * width + lax.broadcasted_iota(jnp.int32, (width,), 0)
    hit = cells[:, None] == cell_ids[None, :]
    return jnp.where(hit[:, None, :], wave[:, :, None], jnp.zeros((), jnp.float32))


def block_solve(previous, cells, wave, owner, lower_full, coupling_full):
    width = lower_full.shape[0]
    term = source_block(cells, wave, owner, width)
    reduced = (term - complex_apply(previous, coupling_full)).astype(jnp.bfloat16)
    return complex_apply(reduced, lower_full)


def per_device(
    lower_inverse,
    coupling,
    source_cell,
    source_wave,
    inflow_field,
    receiver_cell,
    observed,
    adjoint,
):
    owner = lax.axis_index("fac")
    fac_count = lax.axis_size("fac")
    width = lower_inverse.shape[3]
    sources = source_cell.shape[0]
    whole_lower, whole_coupling = (
        lax.all_gather(lower_inverse, "src", axis=1, tiled=True),
        lax.all_gather(coupling, "src", axis=1, tiled=True),
    )
    lower_full = whole_lower[0]
    coupling_full = whole_coupling[0]
    empty_field = jnp.zeros((sources, 2, width), jnp.float32)

    def section_step(section, carry):
        current, received = carry

        def compute():
            return block_solve(received, source_cell, source_wave, owner, lower_full, coupling_full)

        def unchanged():
            return current

        current = lax.cond(section == owner, compute, unchanged)
        received = from_behind(current.astype(jnp.bfloat16), "fac", 1)
        return (current, received)

    current, received = lax.fori_loop(0, fac_count, section_step, (empty_field, inflow_field))
    local_ids = receiver_cell - owner * width
    inside = (local_ids >= 0) & (local_ids < width)
    clipped = jnp.clip(local_ids, 0, width - 1)
    index_both = jnp.broadcast_to(clipped[:, None, :], observed.shape)
    values = jnp.take_along_axis(current, index_both, axis=2)
    values = jnp.where(inside[:, None, :], values, jnp.zeros((), jnp.float32))
    picked = lax.psum(values.astype(jnp.bfloat16), "fac").astype(jnp.float32)
    scale = 1.0 / math.sqrt(sources * lax.axis_size("src"))
    terms = jnp.sum(current * adjoint[:, 0].astype(jnp.float32), axis=(0, 1)) * scale
    gradient = lax.psum_scatter(terms[None, :], "src", scatter_dimension=1, tiled=True)
    return (current[:, None], picked - observed, gradient)


def solution(mesh):
    placed = (
        P("fac", "src", None, None),
        P("fac", "src", None, None),
        P("src"),
        P("src", None),
        P("src", None, None),
        P("src", None),
        P("src", None, None),
        P("src", "fac", None, None),
    )
    return jax.shard_map(
        per_device,
        mesh=mesh,
        in_specs=placed,
        out_specs=(P("src", "fac", None, None), P("src", None, None), P("fac", "src")),
        check_vma=False,
    )
```

profile of v0, /device:TPU:1, one launch (start us, length us, event | category | flops | bytes accessed | tf_op | source)
XLA Modules:
  0.0 633.6 jit_solution(11561115548110792899)
XLA Ops:
  7.2 0.0 all-gather.5.cloned.1.call-start
  7.2 0.7 all-gather.5.cloned.1.call-update
  7.9 0.0 all-gather.3.cloned.1.call-start
  7.9 0.7 all-gather.3.cloned.1.call-update
  8.6 0.0 reduce-scatter.4.cloned.1.call-start
  8.7 1.1 copy.19
  9.9 0.9 broadcast_add_fusion
  10.7 0.9 compare_and_fusion
  11.6 0.2 shift-left_or_fusion
  11.8 76.0 %all-gather.5.cloned.1.call-done = bf16[1,1024,2,1024]{3,2,0,1:T(2,128)(2,1)} async-done(((bf16[1,64,2,1024]{3,2,0,1:T(2,128)(2,1)}), bf16[1,1024,2,1024]{3,2,0,1:T(2,128)(2,1)}) %all-gather.5.cloned.1.call-update) | async-done | bytes 4194320 | tf_op jit(solution)/shard_map/all_gather | solution.py:54
  87.8 77.5 %all-gather.3.cloned.1.call-done = bf16[1,1024,2,1024]{3,2,0,1:T(2,128)(2,1)} async-done(((bf16[1,64,2,1024]{3,2,0,1:T(2,128)(2,1)}), bf16[1,1024,2,1024]{3,2,0,1:T(2,128)(2,1)}) %all-gather.3.cloned.1.call-update) | async-done | bytes 4194320 | tf_op jit(solution)/shard_map/all_gather | solution.py:55
  165.3 0.1 broadcast_in_dim.64
  165.4 56.1 %while.18 = (s32[]{:T(128)}, f32[128,2,1024]{2,0,1:T(8,128)S(1)}, bf16[128,2,1024]{2,0,1:T(8,128)(2,1)S(1)}, s32[]{:T(128)}, s32[128]{0:T(128)}, /*index=5*/f32[...) while((s32[]{:T(128)}, f32[128,2,1024]{2,0,1:T(8,128)S(1)}, ...), condition=%wide.region_3.4_spmd, body=%wide.region_0.3_spmd.sunk | while | flops 2154169344 | bytes 39597816 | solution.py:74
  165.4 0.1 convert_element_type.40
  165.5 1.3 collective-permute-start
  166.8 27.0 %collective-permute-done = bf16[128,2,1024]{2,0,1:T(8,128)(2,1)S(1)} collective-permute-done((bf16[128,2,1024]{2,0,1:T(8,128)(2,1)S(1)}, bf16[128,2,1024]{2,0,1:T(8,128)(2,1)S(1)}, u32[]{:S(2)}, u32[]{:S(2)}) %collective-permute-start) | collective-permute-done | bytes 524320 | tf_op jit(solution)/shard_map/while/body/eval_jaxpr/ppermute | solution.py:12
  193.8 23.8 %conditional.2 = (f32[128,2,1024]{2,0,1:T(8,128)S(1)}) conditional(s32[]{:T(128)} %convert_element_type.39, f32[128,2,1024]{2,0,1:T(8,128)S(1)} %get-tuple-element.280, (s32[128]{0:T(128)}, s32[]{:T(128)}, f32[128,2]{0,1:T(2,128)}, bf16[128,2,1024]{2,0,1:T(8,128)(2,1)S(1)}, bf16[1,1024,2,1024]{3,2,1,0:T(2,128)(2,1)}, ...), branch_computations={%region_1.0_spmd, %region_2.2_spmd} | conditional | flops 2153907200 | bytes 35927604 | solution.py:70
  193.8 0.8 broadcast_compare_fusion
  194.7 0.1 maximum_bitcast_fusion
  194.8 0.0 copy-start.2
  194.8 7.8 %reshape.71 = bf16[1024,2048,1]{1,0,2:T(8,128)(2,1)} reshape(bf16[1,1024,2,1024]{3,2,1,0:T(2,128)(2,1)} %get-tuple-element.153) | data formatting | bytes 8388608 | tf_op jit(solution)/shard_map/while/body/eval_jaxpr/cond/branch_1_fun/reshape;squeeze | solution.py:17
  202.6 0.0 copy-done.2
  202.6 3.5 fusion
  206.2 0.1 maximum_bitcast_fusion.2
  206.3 7.8 %reshape.72 = bf16[1024,2048,1]{1,0,2:T(8,128)(2,1)} reshape(bf16[1,1024,2,1024]{3,2,1,0:T(2,128)(2,1)} %get-tuple-element.154) | data formatting | bytes 8388608 | tf_op jit(solution)/shard_map/while/body/eval_jaxpr/cond/branch_1_fun/reshape;squeeze | solution.py:17
  214.1 3.5 fusion.4
  217.6 0.1 convert_element_type.40
  217.6 1.3 collective-permute-start
  218.9 2.5 collective-permute-done
  221.4 0.0 copy-start
  221.5 310.7 %gather_fusion = bf16[32768]{0:T(1024)(128)(2,1)S(1)} fusion(f32[128,2,1024]{2,0,1:T(8,128)S(1)} %get-tuple-element.168, s32[32768]{0:T(1024)S(1)} %bitcast.40), kind=kCustom, calls=%fused_computation | custom fusion | bytes 524288 | tf_op jit(solution)/shard_map/jit(take_along_axis)/gather | solution.py:79
  532.1 0.0 copy-done
  532.2 0.0 copy-start.1
  532.2 0.2 fusion.12
  532.4 1.0 copy.24
  533.4 0.0 reduce-scatter.4.cloned.1.call-update
  533.4 0.0 all-reduce.2.cloned.1.call-start
  533.5 0.9 fusion.14
  534.4 0.0 all-reduce.2.cloned.1.call-update
  534.4 1.8 copy.28
  536.2 59.9 %reduce-scatter.4.cloned.1.call-done = f32[64,1]{1,0:T(8,128)} async-done(((f32[1024,1]{1,0:T(8,128)}), f32[64,1]{1,0:T(8,128)}) %reduce-scatter.4.cloned.1.call-update) | async-done | bytes 272
  596.1 1.3 copy.25
  597.4 28.1 %all-reduce.2.cloned.1.call-done = bf16[128,2,128]{2,1,0:T(2,128)(2,1)} async-done(((bf16[128,2,128]{2,1,0:T(2,128)(2,1)}), bf16[128,2,128]{2,1,0:T(2,128)(2,1)}) %all-reduce.2.cloned.1.call-update) | async-done | bytes 65552 | tf_op jit(solution)/shard_map/psum | solution.py:81
  625.6 0.0 copy-done.1
  625.6 1.5 convert_subtract_fusion
  (7 shorter events, 0.1 us)
Async XLA Ops:
  7.2 80.6 %all-gather.5.cloned.1.call-start = ((), (), s32[]{:S(2)}) async-start(), calls=%async_computation.2 | async-start | bytes 4456448 | tf_op jit(solution)/shard_map/all_gather | solution.py:54
  7.9 157.4 %all-gather.3.cloned.1.call-start = ((), (), s32[]{:S(2)}) async-start(), calls=%async_computation.1 | async-start | bytes 4456448 | tf_op jit(solution)/shard_map/all_gather | solution.py:55
  8.6 587.5 %reduce-scatter.4.cloned.1.call-start = ((), (), s32[]{:S(2)}) async-start(), calls=%async_computation.4 | async-start | bytes 557056
  165.5 28.3 %collective-permute-start = (bf16[128,2,1024]{2,0,1:T(8,128)(2,1)S(1)}, bf16[128,2,1024]{2,0,1:T(8,128)(2,1)S(1)}, u32[]{:S(2)}, u32[]{:S(2)}) collective-permute-start(bf16[128,2,1024]{2,0,1:T(8,128)(2,1)S(1)} %convert_element_type.40), channel_id=1, source_target_pairs={{0,1},{2,3},{4,5},{6,7},{8,9},{10,11},{12,13},{14,15},{16,17},{18,... | collective-permute-start | bytes 1572872 | tf_op jit(solution)/shard_map/while/body/eval_jaxpr/ppermute | solution.py:12
  194.8 7.8 %copy-start.2 = (f32[128,2]{0,1:T(2,128)S(1)}, f32[128,2]{0,1:T(2,128)}, u32[]{:S(2)}) copy-start(f32[128,2]{0,1:T(2,128)} %get-tuple-element.151) | copy-start | bytes 3076 | tf_op jit(solution)/shard_map/while/body/eval_jaxpr/cond
  217.6 3.8 collective-permute-start
  221.4 310.7 %copy-start = (bf16[128,1,2,1024]{3,2,1,0:T(2,128)(2,1)S(1)}, bf16[128,1,2,1024]{3,2,1,0:T(2,128)(2,1)}, u32[]{:S(2)}) copy-start(bf16[128,1,2,1024]{3,2,1,0:T(2,128)(2,1)} %param.19) | copy-start | bytes 1572868
  532.2 93.4 %copy-start.1 = (f32[128,2,128]{2,1,0:T(2,128)S(1)}, f32[128,2,128]{2,1,0:T(2,128)}, u32[]{:S(2)}) copy-start(f32[128,2,128]{2,1,0:T(2,128)} %param.18) | copy-start | bytes 393220
  533.4 92.1 %all-reduce.2.cloned.1.call-start = ((), (), s32[]{:S(2)}) async-start(), calls=%async_computation.3 | async-start | bytes 131072 | tf_op jit(solution)/shard_map/psum | solution.py:81
Sparse Core Ops, SparseCore 0:
  10.8 76.9 all-gather.4
  90.5 74.6 all-gather.2
  533.6 62.4 reduce-scatter.3
  598.9 26.5 all-reduce.1
where the time goes:
time: 635 us; the launch traced here: 634 us
  local copies, waits for them, and re-layouts  332 us (52%)
  waiting for transfers between devices  272 us (43%)
  between operations  13.8 us (2%)
  matrix products  6.94 us (1%)
    gather x1, local copies, waits for them, and re-layouts, per_device(): values = jnp.take_along_axis(current, index_both, axis=2)  311 us
    all_gather x1, waiting for transfers between devices, per_device(): lax.all_gather(coupling, 'src', axis=1, tiled=True)  77.5 us
    all_gather x1, waiting for transfers between devices, per_device(): lax.all_gather(lower_inverse, 'src', axis=1, tiled=True)  76 us
    unnamed x5, waiting for transfers between devices  61.3 us
    ppermute x2, waiting for transfers between devices, from_behind(): return lax.ppermute(shard, axis, pairs)  29.5 us
    psum x1, waiting for transfers between devices, per_device(): picked = lax.psum(values.astype(jnp.bfloat16), 'fac').astype(jnp.float32)  28.1 us
    another operation x2, local copies, waits for them, and re-layouts, complex_apply(): joined = matrix.reshape(width, 2 * width)  15.7 us
  transfers between devices with their start and end apart: 6, of which 6 were waited for; matrix products, arithmetic and copies ran while one was open for 1% of the time, Pallas kernels for 0%

commit v1 on v0

--- a/solution.py
+++ b/solution.py
@@ -1,9 +1,17 @@
+import functools
 import math
 
 import jax
 import jax.numpy as jnp
 from jax import lax
+from jax.experimental import pallas as pl
+from jax.experimental.pallas import tpu as pltpu
 from jax.sharding import PartitionSpec as P
+
+MESH = pl.DeviceIdType.MESH
+LANES = 128
+UP, DOWN, ACROSS_X, ACROSS_Y = range(4)
+PLANE, LAYERS = 4, 4
 
 
 def from_behind(shard, axis, by):
@@ -36,7 +44,7 @@
     return complex_apply(reduced, lower_full)
 
 
-def per_device(
+def plain_device(
     lower_inverse,
     coupling,
     source_cell,
@@ -85,7 +93,337 @@
     return (current[:, None], picked - observed, gradient)
 
 
+def window_kernel(
+    scale, packed, diagonal, inflow, cell, wave, receivers, observed, adjoint,
+    field, residual, slab,
+    rows_all, diag_all, diag_rows, incoming, reduced, outgoing, terms, terms_all, picked, picked_other,
+    row_send, row_recv, diag_send, diag_recv, term_send, term_recv, pair_send, pair_recv,
+):
+    me, owner = lax.axis_index("src"), lax.axis_index("fac")
+    shards = PLANE * LAYERS
+    x, y, z = me % 2, (me // 2) % 2, me // PLANE
+    x_step, y_step = 1 - 2 * x, 2 - 4 * y
+    _, sources, width = field.shape
+    rows = packed.shape[1]
+    per = LANES // rows
+    tile = min(256, width)
+
+    barrier = pltpu.get_barrier_semaphore()
+
+    @pl.loop(1, shards)
+    def _(offset):
+        pl.semaphore_signal(barrier, inc=1, device_id=((me + offset) % shards, owner), device_id_type=MESH)
+
+    pl.semaphore_signal(barrier, inc=1, device_id=(me, 1 - owner), device_id_type=MESH)
+    pl.semaphore_wait(barrier, shards)
+
+    def row_copy(way, slot, half, target, own=False):
+        return pltpu.make_async_remote_copy(
+            src_ref=packed.at[half] if own else rows_all.at[slot, half],
+            dst_ref=rows_all.at[slot, half],
+            send_sem=row_send.at[way, slot, half],
+            recv_sem=row_recv.at[slot, half],
+            device_id=(target, owner),
+            device_id_type=MESH,
+        )
+
+    def arrived(slot, half):
+        row_copy(ACROSS_X, slot, half, me + x_step).wait_recv()
+
+    def along_z(way, slot, act, own=False):
+        step = PLANE if way == UP else -PLANE
+
+        @pl.when(z < LAYERS - 1 if way == UP else z > 0)
+        def _():
+            for half in range(2):
+                act(row_copy(way, slot, half, me + step, own))
+
+    def in_plane(slot, act, own=False):
+        act(row_copy(ACROSS_X, slot, 0, me + x_step, own))
+        act(row_copy(ACROSS_Y, slot, 1, me + y_step, own))
+        act(row_copy(ACROSS_Y, slot, 0, me + y_step, own))
+        act(row_copy(ACROSS_X, slot, 1, me + x_step, own))
+
+    def relay(slot_x, slot_y, act, wait):
+        if wait:
+            arrived(slot_x, 0)
+        act(row_copy(ACROSS_Y, slot_x, 0, me + y_step))
+        if wait:
+            arrived(slot_y, 1)
+        act(row_copy(ACROSS_X, slot_y, 1, me + x_step))
+
+    def layers_at(step, visit):
+        if step == 0:
+            visit(me, None)
+            return
+
+        @pl.when(z >= step)
+        def _():
+            visit(me - PLANE * step, UP)
+
+        @pl.when(z + step < LAYERS)
+        def _():
+            visit(me + PLANE * step, DOWN)
+
+    def gather_rows(act, wait):
+        def first(slot, way):
+            if way is None:
+                along_z(UP, slot, act, True)
+                along_z(DOWN, slot, act, True)
+                in_plane(slot, act, True)
+                return
+            if wait:
+                arrived(slot, 0)
+                arrived(slot, 1)
+            along_z(way, slot, act)
+            in_plane(slot, act)
+
+        def second(slot, way):
+            relay(slot + x_step, slot + y_step, act, wait)
+
+        layers_at(0, first)
+        for step in range(1, LAYERS):
+            layers_at(step, first)
+            layers_at(step - 1, second)
+        layers_at(LAYERS - 1, second)
+
+    def diag_copy(offset, sender, target):
+        return pltpu.make_async_remote_copy(
+            src_ref=diagonal, dst_ref=diag_all.at[sender],
+            send_sem=diag_send.at[offset], recv_sem=diag_recv.at[sender],
+            device_id=(target, owner), device_id_type=MESH,
+        )
+
+    def term_copy(offset, sender, target):
+        return pltpu.make_async_remote_copy(
+            src_ref=terms.at[target // per], dst_ref=terms_all.at[sender],
+            send_sem=term_send.at[offset], recv_sem=term_recv.at[sender],
+            device_id=(target, owner), device_id_type=MESH,
+        )
+
+    def pair_copy(which, source, target):
+        return pltpu.make_async_remote_copy(
+            src_ref=source, dst_ref=target,
+            send_sem=pair_send.at[which], recv_sem=pair_recv.at[which],
+            device_id=(me, 1 - owner), device_id_type=MESH,
+        )
+
+    def to_all(make):
+        @pl.loop(1, shards)
+        def _(offset):
+            make(offset, me, (me + offset) % shards).start()
+
+    def wait_all(make):
+        @pl.loop(1, shards)
+        def _(offset):
+            other = (me + offset) % shards
+            make(offset, other, other).wait_recv()
+            make(offset, me, other).wait_send()
+
+    to_all(diag_copy)
+    rows_all[me] = packed[...]
+    diag_all[me] = diagonal[...]
+    gather_rows(lambda copy: copy.start(), True)
+    wait_all(diag_copy)
+    for block in range(width // LANES):
+        total = diag_all[block * per].astype(jnp.float32)
+        for other in range(1, per):
+            total += diag_all[block * per + other].astype(jnp.float32)
+        diag_rows[:, block * LANES:(block + 1) * LANES] = total
+
+    for layer in range(LAYERS):
+        slot = me % PLANE + layer * PLANE
+        arrived(slot + x_step, 1)
+        arrived(slot + y_step, 0)
+        arrived(slot + x_step + y_step, 0)
+        arrived(slot + x_step + y_step, 1)
+
+    handover = pair_copy(0, outgoing, incoming)
+
+    @pl.when(owner == 0)
+    def _():
+        incoming[...] = inflow[...]
+
+    @pl.when(owner > 0)
+    def _():
+        handover.wait_recv()
+
+    contract = (((1,), (1,)), ((), ()))
+
+    def matrix_tile(step, half):
+        group = rows_all[pl.ds(step * (tile // rows), tile // rows), half]
+        return group.reshape(tile, width)
+
+    def masks(step):
+        row = lax.broadcasted_iota(jnp.int32, (tile, width), 0) + step * tile
+        return lax.broadcasted_iota(jnp.int32, (tile, width), 1), row
+
+    def product(vector, first, second):
+        with_first = lax.dot_general(vector, first, contract, preferred_element_type=jnp.float32)
+        with_second = lax.dot_general(vector, second, contract, preferred_element_type=jnp.float32)
+        return (
+            with_first[:sources] - with_second[sources:],
+            with_second[:sources] + with_first[sources:],
+        )
+
+    zero = jnp.zeros((), jnp.bfloat16)
+
+    @pl.loop(0, width // tile)
+    def _(step):
+        column, row = masks(step)
+        keep = column >= row
+        parts = product(
+            incoming[...].reshape(2 * sources, width),
+            jnp.where(keep, matrix_tile(step, 0), zero),
+            jnp.where(keep, matrix_tile(step, 1), zero),
+        )
+        at = pl.ds(pl.multiple_of(step * tile, tile), tile)
+        ids = lax.broadcasted_iota(jnp.int32, (sources, tile), 1) + (owner * width + step * tile)
+        hit = ids == cell[...]
+        for part in range(2):
+            term = jnp.where(hit, wave[part], 0.0)
+            reduced[part, :, at] = (term - parts[part]).astype(jnp.bfloat16)
+
+    @pl.loop(0, width // tile)
+    def _(step):
+        column, row = masks(step)
+        keep = column < row
+        real, imag = product(
+            reduced[...].reshape(2 * sources, width),
+            jnp.where(keep, matrix_tile(step, 0), zero),
+            jnp.where(keep, matrix_tile(step, 1), zero),
+        )
+        at = pl.ds(pl.multiple_of(step * tile, tile), tile)
+        red_real, red_imag = (reduced[part, :, at].astype(jnp.float32) for part in range(2))
+        diag_real, diag_imag = diag_rows[0:1, at], diag_rows[1:2, at]
+        real = real + (red_real * diag_real - red_imag * diag_imag)
+        imag = imag + (red_real * diag_imag + red_imag * diag_real)
+        field[0, :, at] = real
+        field[1, :, at] = imag
+        outgoing[0, :, at] = real.astype(jnp.bfloat16)
+        outgoing[1, :, at] = imag.astype(jnp.bfloat16)
+        total = real * adjoint[0, :, at].astype(jnp.float32) + imag * adjoint[1, :, at].astype(jnp.float32)
+        total = jnp.sum(total.reshape(sources // 8, 8, tile), axis=0) * scale
+        for block in range(tile // LANES):
+            terms[step * (tile // LANES) + block] = total[:, block * LANES:(block + 1) * LANES]
+
+    @pl.when(owner == 0)
+    def _():
+        handover.start()
+
+    to_all(term_copy)
+    local = receivers[...] - owner * width
+    lane = local & (LANES - 1)
+    home = local >> (LANES.bit_length() - 1)
+    for part in range(2):
+        values = jnp.zeros((sources, LANES), jnp.float32)
+        for block in range(width // LANES):
+            piece = field[part, :, block * LANES:(block + 1) * LANES]
+            taken = jnp.take_along_axis(piece, lane, axis=1, mode="promise_in_bounds")
+            values = jnp.where(home == block, taken, values)
+        picked[part] = values.astype(jnp.bfloat16)
+    swap = pair_copy(1, picked, picked_other)
+    swap.start()
+
+    wait_all(term_copy)
+    total = terms[me // per]
+    for offset in range(1, shards):
+        total += terms_all[(me + offset) % shards]
+    slab[...] = total
+
+    gather_rows(lambda copy: copy.wait_send(), False)
+
+    @pl.when(owner == 0)
+    def _():
+        handover.wait_send()
+
+    swap.wait()
+    both = picked[...].astype(jnp.float32) + picked_other[...].astype(jnp.float32)
+    residual[...] = both - observed[...]
+
+
+def per_device(
+    lower_inverse,
+    coupling,
+    source_cell,
+    source_wave,
+    inflow_field,
+    receiver_cell,
+    observed,
+    adjoint,
+):
+    me = lax.axis_index("src")
+    shards = lax.axis_size("src")
+    _, rows, _, width = lower_inverse.shape
+    sources, receivers = receiver_cell.shape
+    row_ids = me * rows + lax.broadcasted_iota(jnp.int32, (rows, width), 0)
+    col_ids = lax.broadcasted_iota(jnp.int32, (rows, width), 1)
+    lower = jnp.transpose(lower_inverse[0], (1, 0, 2))
+    packed = jnp.where(col_ids < row_ids, lower, jnp.transpose(coupling[0], (1, 0, 2)))
+    square = lax.dynamic_slice_in_dim(lower_inverse[0], me * rows, rows, axis=2)
+    line = jnp.arange(rows)
+    own = jnp.where((line[:, None] == line[None, :])[:, None, :], square, jnp.zeros((), square.dtype))
+    own = jnp.sum(own.astype(jnp.float32), axis=0).astype(jnp.bfloat16)
+    per = LANES // rows
+    diagonal = lax.dynamic_update_slice(
+        jnp.zeros((16, LANES), jnp.bfloat16), own, (jnp.int32(0), (me % per) * rows)
+    )
+    both = (2, sources, width)
+    dma = pltpu.SemaphoreType.DMA
+    vmem = pl.BlockSpec(memory_space=pltpu.VMEM)
+    scale = 1.0 / math.sqrt(sources * shards)
+    field, residual, slab = pl.pallas_call(
+        functools.partial(window_kernel, scale),
+        out_shape=(
+            jax.ShapeDtypeStruct(both, jnp.float32),
+            jax.ShapeDtypeStruct((2, sources, receivers), jnp.float32),
+            jax.ShapeDtypeStruct((8, LANES), jnp.float32),
+        ),
+        in_specs=[vmem] * 8,
+        out_specs=(vmem,) * 3,
+        scratch_shapes=[
+            pltpu.VMEM((shards, 2, rows, width), jnp.bfloat16),
+            pltpu.VMEM((shards, 16, LANES), jnp.bfloat16),
+            pltpu.VMEM((16, width), jnp.float32),
+            pltpu.VMEM(both, jnp.bfloat16),
+            pltpu.VMEM(both, jnp.bfloat16),
+            pltpu.VMEM(both, jnp.bfloat16),
+            pltpu.VMEM((width // LANES, 8, LANES), jnp.float32),
+            pltpu.VMEM((shards, 8, LANES), jnp.float32),
+            pltpu.VMEM((2, sources, LANES), jnp.bfloat16),
+            pltpu.VMEM((2, sources, LANES), jnp.bfloat16),
+            dma((4, shards, 2)),
+            dma((shards, 2)),
+            dma((shards,)),
+            dma((shards,)),
+            dma((shards,)),
+            dma((shards,)),
+            dma((2,)),
+            dma((2,)),
+        ],
+        compiler_params=pltpu.CompilerParams(
+            collective_id=0, has_side_effects=True, vmem_limit_bytes=48 * 1024 * 1024
+        ),
+    )(
+        packed,
+        diagonal,
+        jnp.transpose(inflow_field, (1, 0, 2)),
+        source_cell[:, None],
+        jnp.transpose(source_wave)[:, :, None],
+        receiver_cell,
+        jnp.transpose(observed, (1, 0, 2)),
+        jnp.transpose(adjoint[:, 0], (1, 0, 2)),
+    )
+    gradient = lax.dynamic_slice_in_dim(jnp.sum(slab, axis=0), (me % per) * rows, rows)
+    return (
+        jnp.transpose(field, (1, 0, 2))[:, None],
+        jnp.transpose(residual, (1, 0, 2)),
+        gradient[None],
+    )
+
+
 def solution(mesh):
+    fits = mesh.shape["src"] == PLANE * LAYERS and mesh.shape["fac"] == 2
     placed = (
         P("fac", "src", None, None),
         P("fac", "src", None, None),
@@ -97,7 +435,7 @@
         P("src", "fac", None, None),
     )
     return jax.shard_map(
-        per_device,
+        per_device if fits else plain_device,
         mesh=mesh,
         in_specs=placed,
         out_specs=(P("src", "fac", None, None), P("src", None, None), P("fac", "src")),

time: 635 us -> 67.3 us (0.11)
  local copies, waits for them, and re-layouts: 332 us -> 6.74 us
  waiting for transfers between devices: 272 us -> 0 us
  Pallas kernels: 0 us -> 58.2 us
  between operations: 13.8 us -> 0.8 us
  matrix products: 6.94 us -> 0 us
    gather x1 -> x0, local copies, waits for them, and re-layouts: 311 us -> none  [per_device(): values = jnp.take_along_axis(current, index_both, axis=2)]
    all_gather x2 -> x0, waiting for transfers between devices: 153 us -> none  [the longest x1 77.5 us: per_device(): lax.all_gather(coupling, 'src', axis=1, tiled=True)]
    unnamed x5 -> x0, waiting for transfers between devices: 61.3 us -> none
    pallas_call x0 -> x1, Pallas kernels: none -> 58.2 us  [per_device(): pl.pallas_call(functools.partial(window_kernel, scale), out_shape=(jax.Sh...]
    ppermute x2 -> x0, waiting for transfers between devices: 29.5 us -> none  [from_behind(): return lax.ppermute(shard, axis, pairs)]
    psum x1 -> x0, waiting for transfers between devices: 28.1 us -> none  [per_device(): picked = lax.psum(values.astype(jnp.bfloat16), 'fac').astype(jnp.float32)]
    another operation x2 -> x0, local copies, waits for them, and re-layouts: 15.7 us -> none  [complex_apply(): joined = matrix.reshape(width, 2 * width)]
    dot_general x2 -> x0, matrix products: 6.94 us -> none  [complex_apply(): lax.dot_general(stacked, joined, contract_dims, preferred_element_type=jn...]
  transfers between devices with their start and end apart: 6 -> 0, of which waited for: 6 -> 0; matrix products, arithmetic and copies ran while one was open for 1% -> 0% of each run, Pallas kernels for 0% -> 0%
where the time goes in v1:
time: 67.3 us; the launch traced here: 67 us
  Pallas kernels  58.2 us (86%)
  local copies, waits for them, and re-layouts  6.74 us (10%)
  other arithmetic  1.21 us (2%)
  between operations  0.8 us (1%)
    pallas_call x1, Pallas kernels, per_device(): pl.pallas_call(functools.partial(window_kernel, scale), out_shape=(jax.Sh...  58.2 us
    unnamed x19, local copies, waits for them, and re-layouts  5.6 us

profile of v1, /device:TPU:1, one launch (start us, length us, event | category | flops | bytes accessed | tf_op | source)
XLA Modules:
  0.0 67.0 jit_solution(9477438066322422882)
XLA Ops:
  0.7 0.9 %fusion.1 = bf16[2,64]{1,0:T(2,128)(2,1)S(1)} fusion(pred[64,64]{1,0:T(8,128)(4,1)S(1)} %iota_compare_fusion.1, bf16[1,64,2,1024]{3,2,1,0:T(2,128)(2,1)} %param.8, s32[]{:T(128)S(6)} %select_n.28), kind=kLoop, calls=%fused_computation.7 | loop fusion | flops 16256 | bytes 20740 | tf_op jit(solution)/shard_map/reduce_sum | solution.py:366
  1.6 0.0 copy-start.5
  1.6 0.0 copy-start.6
  1.6 0.3 dynamic_update_slice.3.diagonal
  1.9 0.0 copy-start.3
  1.9 0.0 copy-start.4
  2.0 0.1 iota_compare_fusion
  2.1 0.2 copy-done.6
  2.3 0.1 copy.24.cell
  2.4 0.0 copy-done.5
  2.4 0.1 copy.25.wave
  2.5 0.0 copy-start.1
  2.5 1.0 %copy.35 = f32[128,2,128]{2,0,1:T(8,128)S(1)} copy(f32[128,2,128]{2,1,0:T(2,128)} %param.14) | data formatting | bytes 262144 | tf_op args[6]
  3.5 0.0 copy-done.3
  3.5 0.0 copy-done.4
  3.5 0.2 fusion.packed
  3.7 0.0 copy-done.1
  3.7 0.0 copy-start.2
  3.7 0.1 copy.34
  3.8 0.9 %copy-done.2 = bf16[128,1,2,1024]{3,2,1,0:T(2,128)(2,1)S(1)} copy-done((bf16[128,1,2,1024]{3,2,1,0:T(2,128)(2,1)S(1)}, bf16[128,1,2,1024]{3,2,1,0:T(2,128)(2,1)}, u32[]{:S(2)}) %copy-start.2) | copy-done | bytes 524312
  4.8 0.0 copy-start
  4.8 0.1 copy.33
  4.9 0.7 %copy-done = s32[128,128]{1,0:T(8,128)S(1)} copy-done((s32[128,128]{1,0:T(8,128)S(1)}, s32[128,128]{1,0:T(8,128)}, u32[]{:S(2)}) %copy-start) | copy-done | bytes 65560
  5.6 58.2 %shard_map.103 = (f32[2,128,1024]{2,1,0:T(8,128)S(1)}, f32[2,128,128]{2,1,0:T(8,128)S(1)}, f32[8,128]{1,0:T(8,128)S(1)}) custom-call(bf16[2,64,1024]{2,1,0:T(8,128)(2,1)S(1)} %fusion.packed, bf16[16,128]{1,0:T(8,128)(2,1)S(1)} %dynamic_update_slice.3.diagonal, bf16[2,128,1024]{2,1,0:T(8,128)(2,1)S(1)} %bitcast.31, s32[128,1]{1,0:T(8,128)S(1)} %copy.24.cell, ...), custom_call_target="tpu_custom_call" | custom-call | tf_op jit(solution)/shard_map/pallas_call | solution.py:375
  63.9 1.8 %copy.26 = f32[128,1,2,1024]{3,2,1,0:T(2,128)} copy(f32[128,1,2,1024]{3,0,2,1:T(8,128)S(1)} %bitcast.33) | data formatting | bytes 2097152
  65.6 0.8 %copy.27 = f32[128,2,128]{2,1,0:T(2,128)} copy(f32[128,2,128]{2,0,1:T(8,128)S(1)} %bitcast.35) | data formatting | bytes 262144
  66.4 0.6 dynamic-slice_bitcast_fusion
  (4 shorter events, 0.0 us)
Async XLA Ops:
  1.6 0.8 %copy-start.5 = (f32[128,2]{0,1:T(2,128)S(1)}, f32[128,2]{0,1:T(2,128)}, u32[]{:S(2)}) copy-start(f32[128,2]{0,1:T(2,128)} %param.11) | copy-start | bytes 3076
  1.6 0.7 copy-start.6
  1.9 1.6 %copy-start.3 = (bf16[1,64,2,1024]{3,2,1,0:T(2,128)(2,1)S(1)}, bf16[1,64,2,1024]{3,2,1,0:T(2,128)(2,1)}, u32[]{:S(2)}) copy-start(bf16[1,64,2,1024]{3,2,1,0:T(2,128)(2,1)} %param.8) | copy-start | bytes 786436
  1.9 1.6 %copy-start.4 = (bf16[1,64,2,1024]{3,2,1,0:T(2,128)(2,1)S(1)}, bf16[1,64,2,1024]{3,2,1,0:T(2,128)(2,1)}, u32[]{:S(2)}) copy-start(bf16[1,64,2,1024]{3,2,1,0:T(2,128)(2,1)} %param.9) | copy-start | bytes 786436
  2.5 1.2 %copy-start.1 = (bf16[128,2,1024]{2,1,0:T(2,128)(2,1)S(1)}, bf16[128,2,1024]{2,1,0:T(2,128)(2,1)}, u32[]{:S(2)}) copy-start(bf16[128,2,1024]{2,1,0:T(2,128)(2,1)} %param.12) | copy-start | bytes 1572868
  3.7 1.0 %copy-start.2 = (bf16[128,1,2,1024]{3,2,1,0:T(2,128)(2,1)S(1)}, bf16[128,1,2,1024]{3,2,1,0:T(2,128)(2,1)}, u32[]{:S(2)}) copy-start(bf16[128,1,2,1024]{3,2,1,0:T(2,128)(2,1)} %param.15) | copy-start | bytes 1572868
  4.8 0.8 %copy-start = (s32[128,128]{1,0:T(8,128)S(1)}, s32[128,128]{1,0:T(8,128)}, u32[]{:S(2)}) copy-start(s32[128,128]{1,0:T(8,128)} %receivers.1) | copy-start | bytes 196612

commit v2 on v1

--- a/solution.py
+++ b/solution.py
@@ -97,7 +97,7 @@
     scale, packed, diagonal, inflow, cell, wave, receivers, observed, adjoint,
     field, residual, slab,
     rows_all, diag_all, diag_rows, incoming, reduced, outgoing, terms, terms_all, picked, picked_other,
-    row_send, row_recv, diag_send, diag_recv, term_send, term_recv, pair_send, pair_recv,
+    row_send, row_recv, diag_send, diag_recv, term_send, term_recv, pair_send, pair_recv, turn,
 ):
     me, owner = lax.axis_index("src"), lax.axis_index("fac")
     shards = PLANE * LAYERS
@@ -106,7 +106,7 @@
     _, sources, width = field.shape
     rows = packed.shape[1]
     per = LANES // rows
-    tile = min(256, width)
+    tile = PLANE * rows
 
     barrier = pltpu.get_barrier_semaphore()
 
@@ -223,7 +223,17 @@
     to_all(diag_copy)
     rows_all[me] = packed[...]
     diag_all[me] = diagonal[...]
+
+    @pl.when(owner > 0)
+    def _():
+        pl.semaphore_wait(turn, 1)
+
     gather_rows(lambda copy: copy.start(), True)
+
+    @pl.when(owner == 0)
+    def _():
+        pl.semaphore_signal(turn, inc=1, device_id=(me, 1 - owner), device_id_type=MESH)
+
     wait_all(diag_copy)
     for block in range(width // LANES):
         total = diag_all[block * per].astype(jnp.float32)
@@ -231,69 +241,60 @@
             total += diag_all[block * per + other].astype(jnp.float32)
         diag_rows[:, block * LANES:(block + 1) * LANES] = total
 
+    handover = pair_copy(0, outgoing, incoming)
+
+    @pl.when(owner == 0)
+    def _():
+        incoming[...] = inflow[...]
+
+    @pl.when(owner > 0)
+    def _():
+        handover.wait_recv()
+
+    contract = (((1,), (1,)), ((), ()))
+
+    def product(vector, layer, half, keep, others):
+        group = rows_all.at[layer * PLANE:(layer + 1) * PLANE, half]
+        middle = slice(layer * tile, (layer + 1) * tile)
+        square = jnp.where(keep, group[:, :, middle].reshape(tile, tile), jnp.zeros((), jnp.bfloat16))
+        total = lax.dot_general(
+            vector[:, :, middle].reshape(2 * sources, tile), square, contract,
+            preferred_element_type=jnp.float32,
+        )
+        if others.start < others.stop:
+            count = others.stop - others.start
+            total += lax.dot_general(
+                vector[:, :, others].reshape(2 * sources, count),
+                group[:, :, others].reshape(tile, count), contract,
+                preferred_element_type=jnp.float32,
+            )
+        return total
+
+    def complex_product(vector, layer, keep, others):
+        real = product(vector, layer, 0, keep, others)
+        imag = product(vector, layer, 1, keep, others)
+        return real[:sources] - imag[sources:], imag[:sources] + real[sources:]
+
+    row = lax.broadcasted_iota(jnp.int32, (tile, tile), 0)
+    column = lax.broadcasted_iota(jnp.int32, (tile, tile), 1)
+
     for layer in range(LAYERS):
         slot = me % PLANE + layer * PLANE
         arrived(slot + x_step, 1)
         arrived(slot + y_step, 0)
         arrived(slot + x_step + y_step, 0)
         arrived(slot + x_step + y_step, 1)
-
-    handover = pair_copy(0, outgoing, incoming)
-
-    @pl.when(owner == 0)
-    def _():
-        incoming[...] = inflow[...]
-
-    @pl.when(owner > 0)
-    def _():
-        handover.wait_recv()
-
-    contract = (((1,), (1,)), ((), ()))
-
-    def matrix_tile(step, half):
-        group = rows_all[pl.ds(step * (tile // rows), tile // rows), half]
-        return group.reshape(tile, width)
-
-    def masks(step):
-        row = lax.broadcasted_iota(jnp.int32, (tile, width), 0) + step * tile
-        return lax.broadcasted_iota(jnp.int32, (tile, width), 1), row
-
-    def product(vector, first, second):
-        with_first = lax.dot_general(vector, first, contract, preferred_element_type=jnp.float32)
-        with_second = lax.dot_general(vector, second, contract, preferred_element_type=jnp.float32)
-        return (
-            with_first[:sources] - with_second[sources:],
-            with_second[:sources] + with_first[sources:],
-        )
-
-    zero = jnp.zeros((), jnp.bfloat16)
-
-    @pl.loop(0, width // tile)
-    def _(step):
-        column, row = masks(step)
-        keep = column >= row
-        parts = product(
-            incoming[...].reshape(2 * sources, width),
-            jnp.where(keep, matrix_tile(step, 0), zero),
-            jnp.where(keep, matrix_tile(step, 1), zero),
-        )
-        at = pl.ds(pl.multiple_of(step * tile, tile), tile)
-        ids = lax.broadcasted_iota(jnp.int32, (sources, tile), 1) + (owner * width + step * tile)
+        at = slice(layer * tile, (layer + 1) * tile)
+        parts = complex_product(incoming, layer, column >= row, slice((layer + 1) * tile, width))
+        ids = lax.broadcasted_iota(jnp.int32, (sources, tile), 1) + (owner * width + layer * tile)
         hit = ids == cell[...]
         for part in range(2):
             term = jnp.where(hit, wave[part], 0.0)
             reduced[part, :, at] = (term - parts[part]).astype(jnp.bfloat16)
 
-    @pl.loop(0, width // tile)
-    def _(step):
-        column, row = masks(step)
-        keep = column < row
-        real, imag = product(
-            reduced[...].reshape(2 * sources, width),
-            jnp.where(keep, matrix_tile(step, 0), zero),
-            jnp.where(keep, matrix_tile(step, 1), zero),
-        )
-        at = pl.ds(pl.multiple_of(step * tile, tile), tile)
+    for layer in range(LAYERS):
+        at = slice(layer * tile, (layer + 1) * tile)
+        real, imag = complex_product(reduced, layer, column < row, slice(0, layer * tile))
         red_real, red_imag = (reduced[part, :, at].astype(jnp.float32) for part in range(2))
         diag_real, diag_imag = diag_rows[0:1, at], diag_rows[1:2, at]
         real = real + (red_real * diag_real - red_imag * diag_imag)
@@ -305,7 +306,7 @@
         total = real * adjoint[0, :, at].astype(jnp.float32) + imag * adjoint[1, :, at].astype(jnp.float32)
         total = jnp.sum(total.reshape(sources // 8, 8, tile), axis=0) * scale
         for block in range(tile // LANES):
-            terms[step * (tile // LANES) + block] = total[:, block * LANES:(block + 1) * LANES]
+            terms[layer * (tile // LANES) + block] = total[:, block * LANES:(block + 1) * LANES]
 
     @pl.when(owner == 0)
     def _():
@@ -400,6 +401,7 @@
             dma((shards,)),
             dma((2,)),
             dma((2,)),
+            pltpu.SemaphoreType.REGULAR,
         ],
         compiler_params=pltpu.CompilerParams(
             collective_id=0, has_side_effects=True, vmem_limit_bytes=48 * 1024 * 1024

time: 67.3 us -> 66.7 us (level)
  no operation moved by 1% of the time
where the time goes in v2:
time: 66.7 us; the launch traced here: 66.3 us
  Pallas kernels  57.6 us (86%)
  local copies, waits for them, and re-layouts  6.74 us (10%)
  other arithmetic  1.21 us (2%)
  between operations  0.8 us (1%)
    pallas_call x1, Pallas kernels, per_device(): pl.pallas_call(functools.partial(window_kernel, scale), out_shape=(jax.Sh...  57.6 us
    unnamed x19, local copies, waits for them, and re-layouts  5.6 us

profile of v2, /device:TPU:1, one launch (start us, length us, event | category | flops | bytes accessed | tf_op | source)
XLA Modules:
  0.0 66.3 jit_solution(10627070606930714692)
XLA Ops:
  0.7 0.9 %fusion.1 = bf16[2,64]{1,0:T(2,128)(2,1)S(1)} fusion(pred[64,64]{1,0:T(8,128)(4,1)S(1)} %iota_compare_fusion.1, bf16[1,64,2,1024]{3,2,1,0:T(2,128)(2,1)} %param.8, s32[]{:T(128)S(6)} %select_n.28), kind=kLoop, calls=%fused_computation.7 | loop fusion | flops 16256 | bytes 20740 | tf_op jit(solution)/shard_map/reduce_sum | solution.py:367
  1.6 0.0 copy-start.5
  1.6 0.0 copy-start.6
  1.6 0.3 dynamic_update_slice.3.diagonal
  1.9 0.0 copy-start.3
  1.9 0.0 copy-start.4
  2.0 0.1 iota_compare_fusion
  2.1 0.2 copy-done.6
  2.3 0.1 copy.24.cell
  2.4 0.0 copy-done.5
  2.4 0.1 copy.25.wave
  2.5 0.0 copy-start.1
  2.5 1.0 %copy.35 = f32[128,2,128]{2,0,1:T(8,128)S(1)} copy(f32[128,2,128]{2,1,0:T(2,128)} %param.14) | data formatting | bytes 262144 | tf_op args[6]
  3.5 0.0 copy-done.3
  3.5 0.0 copy-done.4
  3.5 0.2 fusion.packed
  3.7 0.0 copy-done.1
  3.7 0.0 copy-start.2
  3.7 0.1 copy.34
  3.8 0.9 %copy-done.2 = bf16[128,1,2,1024]{3,2,1,0:T(2,128)(2,1)S(1)} copy-done((bf16[128,1,2,1024]{3,2,1,0:T(2,128)(2,1)S(1)}, bf16[128,1,2,1024]{3,2,1,0:T(2,128)(2,1)}, u32[]{:S(2)}) %copy-start.2) | copy-done | bytes 524312
  4.8 0.0 copy-start
  4.8 0.1 copy.33
  4.9 0.7 %copy-done = s32[128,128]{1,0:T(8,128)S(1)} copy-done((s32[128,128]{1,0:T(8,128)S(1)}, s32[128,128]{1,0:T(8,128)}, u32[]{:S(2)}) %copy-start) | copy-done | bytes 65560
  5.6 57.6 %shard_map.103 = (f32[2,128,1024]{2,1,0:T(8,128)S(1)}, f32[2,128,128]{2,1,0:T(8,128)S(1)}, f32[8,128]{1,0:T(8,128)S(1)}) custom-call(bf16[2,64,1024]{2,1,0:T(8,128)(2,1)S(1)} %fusion.packed, bf16[16,128]{1,0:T(8,128)(2,1)S(1)} %dynamic_update_slice.3.diagonal, bf16[2,128,1024]{2,1,0:T(8,128)(2,1)S(1)} %bitcast.31, s32[128,1]{1,0:T(8,128)S(1)} %copy.24.cell, ...), custom_call_target="tpu_custom_call" | custom-call | tf_op jit(solution)/shard_map/pallas_call | solution.py:376
  63.2 1.8 %copy.26 = f32[128,1,2,1024]{3,2,1,0:T(2,128)} copy(f32[128,1,2,1024]{3,0,2,1:T(8,128)S(1)} %bitcast.33) | data formatting | bytes 2097152
  65.0 0.8 %copy.27 = f32[128,2,128]{2,1,0:T(2,128)} copy(f32[128,2,128]{2,0,1:T(8,128)S(1)} %bitcast.35) | data formatting | bytes 262144
  65.8 0.6 dynamic-slice_bitcast_fusion
  (4 shorter events, 0.0 us)
Async XLA Ops:
  1.6 0.8 %copy-start.5 = (f32[128,2]{0,1:T(2,128)S(1)}, f32[128,2]{0,1:T(2,128)}, u32[]{:S(2)}) copy-start(f32[128,2]{0,1:T(2,128)} %param.11) | copy-start | bytes 3076
  1.6 0.7 copy-start.6
  1.9 1.6 %copy-start.3 = (bf16[1,64,2,1024]{3,2,1,0:T(2,128)(2,1)S(1)}, bf16[1,64,2,1024]{3,2,1,0:T(2,128)(2,1)}, u32[]{:S(2)}) copy-start(bf16[1,64,2,1024]{3,2,1,0:T(2,128)(2,1)} %param.8) | copy-start | bytes 786436
  1.9 1.6 %copy-start.4 = (bf16[1,64,2,1024]{3,2,1,0:T(2,128)(2,1)S(1)}, bf16[1,64,2,1024]{3,2,1,0:T(2,128)(2,1)}, u32[]{:S(2)}) copy-start(bf16[1,64,2,1024]{3,2,1,0:T(2,128)(2,1)} %param.9) | copy-start | bytes 786436
  2.5 1.2 %copy-start.1 = (bf16[128,2,1024]{2,1,0:T(2,128)(2,1)S(1)}, bf16[128,2,1024]{2,1,0:T(2,128)(2,1)}, u32[]{:S(2)}) copy-start(bf16[128,2,1024]{2,1,0:T(2,128)(2,1)} %param.12) | copy-start | bytes 1572868
  3.7 1.0 %copy-start.2 = (bf16[128,1,2,1024]{3,2,1,0:T(2,128)(2,1)S(1)}, bf16[128,1,2,1024]{3,2,1,0:T(2,128)(2,1)}, u32[]{:S(2)}) copy-start(bf16[128,1,2,1024]{3,2,1,0:T(2,128)(2,1)} %param.15) | copy-start | bytes 1572868
  4.8 0.8 %copy-start = (s32[128,128]{1,0:T(8,128)S(1)}, s32[128,128]{1,0:T(8,128)}, u32[]{:S(2)}) copy-start(s32[128,128]{1,0:T(8,128)} %receivers.1) | copy-start | bytes 196612

commit v3 on v2

--- a/solution.py
+++ b/solution.py
@@ -94,10 +94,10 @@
 
 
 def window_kernel(
-    scale, packed, diagonal, inflow, cell, wave, receivers, observed, adjoint,
+    scale, packed, diagonal, inflow, cell, wave, receivers_far, adjoint,
     field, residual, slab,
     rows_all, diag_all, diag_rows, incoming, reduced, outgoing, terms, terms_all, picked, picked_other,
-    row_send, row_recv, diag_send, diag_recv, term_send, term_recv, pair_send, pair_recv, turn,
+    row_send, row_recv, diag_send, diag_recv, term_send, term_recv, pair_send, pair_recv, turn, receivers, receivers_done,
 ):
     me, owner = lax.axis_index("src"), lax.axis_index("fac")
     shards = PLANE * LAYERS
@@ -165,7 +165,7 @@
         def _():
             visit(me + PLANE * step, DOWN)
 
-    def gather_rows(act, wait):
+    def gather_rows(act, wait, midway=None):
         def first(slot, way):
             if way is None:
                 along_z(UP, slot, act, True)
@@ -184,6 +184,8 @@
         layers_at(0, first)
         for step in range(1, LAYERS):
             layers_at(step, first)
+            if midway is not None and step == 2:
+                midway()
             layers_at(step - 1, second)
         layers_at(LAYERS - 1, second)
 
@@ -220,6 +222,8 @@
             make(offset, other, other).wait_recv()
             make(offset, me, other).wait_send()
 
+    receivers_copy = pltpu.make_async_copy(receivers_far, receivers, receivers_done)
+    receivers_copy.start()
     to_all(diag_copy)
     rows_all[me] = packed[...]
     diag_all[me] = diagonal[...]
@@ -228,12 +232,12 @@
     def _():
         pl.semaphore_wait(turn, 1)
 
-    gather_rows(lambda copy: copy.start(), True)
-
-    @pl.when(owner == 0)
-    def _():
-        pl.semaphore_signal(turn, inc=1, device_id=(me, 1 - owner), device_id_type=MESH)
-
+    def pass_turn():
+        @pl.when(owner == 0)
+        def _():
+            pl.semaphore_signal(turn, inc=1, device_id=(me, 1 - owner), device_id_type=MESH)
+
+    gather_rows(lambda copy: copy.start(), True, pass_turn)
     wait_all(diag_copy)
     for block in range(width // LANES):
         total = diag_all[block * per].astype(jnp.float32)
@@ -278,7 +282,7 @@
     row = lax.broadcasted_iota(jnp.int32, (tile, tile), 0)
     column = lax.broadcasted_iota(jnp.int32, (tile, tile), 1)
 
-    for layer in range(LAYERS):
+    def reduce_layer(layer):
         slot = me % PLANE + layer * PLANE
         arrived(slot + x_step, 1)
         arrived(slot + y_step, 0)
@@ -291,6 +295,16 @@
         for part in range(2):
             term = jnp.where(hit, wave[part], 0.0)
             reduced[part, :, at] = (term - parts[part]).astype(jnp.bfloat16)
+
+    @pl.when(z < LAYERS // 2)
+    def _():
+        for layer in range(LAYERS):
+            reduce_layer(layer)
+
+    @pl.when(z >= LAYERS // 2)
+    def _():
+        for layer in reversed(range(LAYERS)):
+            reduce_layer(layer)
 
     for layer in range(LAYERS):
         at = slice(layer * tile, (layer + 1) * tile)
@@ -307,12 +321,17 @@
         total = jnp.sum(total.reshape(sources // 8, 8, tile), axis=0) * scale
         for block in range(tile // LANES):
             terms[layer * (tile // LANES) + block] = total[:, block * LANES:(block + 1) * LANES]
+        for target in range(layer * PLANE, (layer + 1) * PLANE):
+
+            @pl.when(me != target)
+            def _(target=target):
+                term_copy(target, me, target).start()
 
     @pl.when(owner == 0)
     def _():
         handover.start()
 
-    to_all(term_copy)
+    receivers_copy.wait()
     local = receivers[...] - owner * width
     lane = local & (LANES - 1)
     home = local >> (LANES.bit_length() - 1)
@@ -326,7 +345,12 @@
     swap = pair_copy(1, picked, picked_other)
     swap.start()
 
-    wait_all(term_copy)
+    @pl.loop(1, shards)
+    def _(offset):
+        other = (me + offset) % shards
+        term_copy(other, other, other).wait_recv()
+        term_copy(other, me, other).wait_send()
+
     total = terms[me // per]
     for offset in range(1, shards):
         total += terms_all[(me + offset) % shards]
@@ -340,7 +364,7 @@
 
     swap.wait()
     both = picked[...].astype(jnp.float32) + picked_other[...].astype(jnp.float32)
-    residual[...] = both - observed[...]
+    residual[...] = both
 
 
 def per_device(
@@ -380,7 +404,7 @@
             jax.ShapeDtypeStruct((2, sources, receivers), jnp.float32),
             jax.ShapeDtypeStruct((8, LANES), jnp.float32),
         ),
-        in_specs=[vmem] * 8,
+        in_specs=[vmem] * 5 + [pl.BlockSpec(memory_space=pl.ANY), vmem],
         out_specs=(vmem,) * 3,
         scratch_shapes=[
             pltpu.VMEM((shards, 2, rows, width), jnp.bfloat16),
@@ -402,6 +426,8 @@
             dma((2,)),
             dma((2,)),
             pltpu.SemaphoreType.REGULAR,
+            pltpu.VMEM((sources, receivers), jnp.int32),
+            dma,
         ],
         compiler_params=pltpu.CompilerParams(
             collective_id=0, has_side_effects=True, vmem_limit_bytes=48 * 1024 * 1024
@@ -413,13 +439,12 @@
         source_cell[:, None],
         jnp.transpose(source_wave)[:, :, None],
         receiver_cell,
-        jnp.transpose(observed, (1, 0, 2)),
         jnp.transpose(adjoint[:, 0], (1, 0, 2)),
     )
     gradient = lax.dynamic_slice_in_dim(jnp.sum(slab, axis=0), (me % per) * rows, rows)
     return (
         jnp.transpose(field, (1, 0, 2))[:, None],
-        jnp.transpose(residual, (1, 0, 2)),
+        jnp.transpose(residual, (1, 0, 2)) - observed,
         gradient[None],
     )
 

time: 66.7 us -> 64.2 us (0.963)
  Pallas kernels: 57.6 us -> 54 us
  other arithmetic: 1.21 us -> 2.21 us
    pallas_call x1, Pallas kernels: 57.6 us -> 54 us  [per_device(): pl.pallas_call(functools.partial(window_kernel, scale), out_shape=(jax.Sh...]
    unnamed x19 -> x14, local copies, waits for them, and re-layouts: 5.6 us -> 4.42 us
    select_n x1, other arithmetic: 0.17 us -> 1.12 us  [per_device(): jnp.where(col_ids < row_ids, lower, jnp.transpose(coupling[0], (1, 0, 2)))]
    broadcast_in_dim x1, local copies, waits for them, and re-layouts: 0.11 us -> 0.82 us  [per_device(): source_cell[:, None]]
    broadcast_in_dim x1, local copies, waits for them, and re-layouts: 0.13 us -> 0.8 us  [per_device(): jnp.transpose(source_wave)[:, :, None]]
where the time goes in v3:
time: 64.2 us; the launch traced here: 63.9 us
  Pallas kernels  54 us (84%)
  local copies, waits for them, and re-layouts  6.93 us (11%)
  other arithmetic  2.21 us (3%)
  between operations  0.77 us (1%)
    pallas_call x1, Pallas kernels, per_device(): pl.pallas_call(functools.partial(window_kernel, scale), out_shape=(jax.Sh...  54 us
    unnamed x14, local copies, waits for them, and re-layouts  4.42 us

profile of v3, /device:TPU:1, one launch (start us, length us, event | category | flops | bytes accessed | tf_op | source)
XLA Modules:
  0.0 63.9 jit_solution(15782912550228971661)
XLA Ops:
  0.6 0.0 copy-start.3
  0.7 0.9 %fusion.1 = bf16[2,64]{1,0:T(2,128)(2,1)S(1)} fusion(pred[64,64]{1,0:T(8,128)(4,1)S(1)} %iota_compare_fusion.1, bf16[1,64,2,1024]{3,2,1,0:T(2,128)(2,1)} %param.8, s32[]{:T(128)S(6)} %select_n.28), kind=kLoop, calls=%fused_computation.7 | loop fusion | flops 16256 | bytes 20740 | tf_op jit(solution)/shard_map/reduce_sum | solution.py:391
  1.6 0.3 dynamic_update_slice.3.diagonal
  1.9 0.1 iota_compare_fusion
  2.1 0.0 copy-start.1
  2.1 0.8 %copy.23.cell = s32[128,1]{1,0:T(8,128)S(1)} copy(s32[128,1]{0,1:T(1,128)} %bitcast.33) | data formatting | bytes 1024 | tf_op jit(solution)/shard_map/broadcast_in_dim | solution.py:439
  2.9 0.8 %copy.24.wave = f32[2,128,1]{2,1,0:T(8,128)S(1)} copy(f32[2,128,1]{1,0,2:T(2,128)} %bitcast.32) | data formatting | bytes 2048 | tf_op jit(solution)/shard_map/broadcast_in_dim | solution.py:440
  3.7 0.0 copy-done.3
  3.7 1.1 %fusion.packed = bf16[2,64,1024]{2,1,0:T(8,128)(2,1)S(1)} fusion(bf16[1,64,2,1024]{3,2,1,0:T(2,128)(2,1)} %param.9, bf16[1,64,2,1024]{3,2,1,0:T(2,128)(2,1)S(1)} %copy-done.3, pred[64,1024]{1,0:T(8,128)(4,1)S(1)} %iota_compare_fusion), kind=kLoop, calls=%fused_computation.3 | loop fusion | flops 131072 | bytes 851968 | tf_op jit(solution)/shard_map/jit(_where)/select_n | solution.py:387
  4.8 0.0 copy-done.1
  4.8 0.0 copy-start.2
  4.9 0.1 copy.34
  5.0 0.9 %copy-done.2 = bf16[128,1,2,1024]{3,2,1,0:T(2,128)(2,1)S(1)} copy-done((bf16[128,1,2,1024]{3,2,1,0:T(2,128)(2,1)S(1)}, bf16[128,1,2,1024]{3,2,1,0:T(2,128)(2,1)}, u32[]{:S(2)}) %copy-start.2) | copy-done | bytes 524312
  5.9 0.0 copy-start
  5.9 0.1 copy.33
  6.0 0.7 %copy-done = s32[128,128]{1,0:T(8,128)S(1)} copy-done((s32[128,128]{1,0:T(8,128)S(1)}, s32[128,128]{1,0:T(8,128)}, u32[]{:S(2)}) %copy-start) | copy-done | bytes 65560
  6.7 54.0 %shard_map.103 = (f32[2,128,1024]{2,1,0:T(8,128)S(1)}, f32[2,128,128]{2,1,0:T(8,128)S(1)}, f32[8,128]{1,0:T(8,128)S(1)}) custom-call(bf16[2,64,1024]{2,1,0:T(8,128)(2,1)S(1)} %fusion.packed, bf16[16,128]{1,0:T(8,128)(2,1)S(1)} %dynamic_update_slice.3.diagonal, bf16[2,128,1024]{2,1,0:T(8,128)(2,1)S(1)} %bitcast.29, s32[128,1]{1,0:T(8,128)S(1)} %copy.23.cell, ...), custom_call_target="tpu_custom_call" | custom-call | tf_op jit(solution)/shard_map/pallas_call | solution.py:400
  60.7 0.0 copy-start.4
  60.8 1.8 %copy.26 = f32[128,1,2,1024]{3,2,1,0:T(2,128)} copy(f32[128,1,2,1024]{3,0,2,1:T(8,128)S(1)} %bitcast.31) | data formatting | bytes 2097152
  62.5 0.6 dynamic-slice_bitcast_fusion
  63.1 0.0 copy-done.4
  63.2 0.8 %copy.27 = f32[128,2,128]{2,1,0:T(2,128)} copy(f32[128,2,128]{2,0,1:T(8,128)S(1)} %bitcast_subtract_fusion) | data formatting | bytes 262144
  (5 shorter events, 0.1 us)
Async XLA Ops:
  0.6 3.1 %copy-start.3 = (bf16[1,64,2,1024]{3,2,1,0:T(2,128)(2,1)S(1)}, bf16[1,64,2,1024]{3,2,1,0:T(2,128)(2,1)}, u32[]{:S(2)}) copy-start(bf16[1,64,2,1024]{3,2,1,0:T(2,128)(2,1)} %param.8) | copy-start | bytes 786436
  2.1 2.8 %copy-start.1 = (bf16[128,2,1024]{2,1,0:T(2,128)(2,1)S(1)}, bf16[128,2,1024]{2,1,0:T(2,128)(2,1)}, u32[]{:S(2)}) copy-start(bf16[128,2,1024]{2,1,0:T(2,128)(2,1)} %param.12) | copy-start | bytes 1572868
  4.8 1.0 %copy-start.2 = (bf16[128,1,2,1024]{3,2,1,0:T(2,128)(2,1)S(1)}, bf16[128,1,2,1024]{3,2,1,0:T(2,128)(2,1)}, u32[]{:S(2)}) copy-start(bf16[128,1,2,1024]{3,2,1,0:T(2,128)(2,1)} %param.15) | copy-start | bytes 1572868
  5.9 0.8 %copy-start = (s32[128,128]{1,0:T(8,128)S(1)}, s32[128,128]{1,0:T(8,128)}, u32[]{:S(2)}) copy-start(s32[128,128]{1,0:T(8,128)} %receivers_far.1) | copy-start | bytes 196612
  60.7 2.4 %copy-start.4 = (f32[128,2,128]{2,1,0:T(2,128)S(1)}, f32[128,2,128]{2,1,0:T(2,128)}, u32[]{:S(2)}) copy-start(f32[128,2,128]{2,1,0:T(2,128)} %param.14) | copy-start | bytes 393220
